TPU v7x, 128 devices: a whole 4x4x4 slice. The times are simulated.
128 devices in a mesh: seq: 8 (over x_hi, z), tp: 16 (over y, x_lo, core).
Axes of the slice: x: 4 (x_hi: 2, x_lo: 2; x = x_hi * 2 + x_lo), y: 4, z: 4, core: 2. Of those that a mesh axis runs over, the one named last changes fastest.
Arguments:
- teacher_hidden: bfloat16 [16384, 16384], P('seq', 'tp'), may hold values from -9 to 9
- teacher_gain: bfloat16 [16384], P('tp'), may hold values from 0.25 to 1.75
- target_proj: bfloat16 [16384, 4096], P('tp'), may hold values from -0.046875 to 0.046875
- student_in: bfloat16 [16384, 4096], P(('seq', 'tp')), may hold values from -6 to 6
- student_gain: bfloat16 [4096], replicated, may hold values from 0.25 to 1.75
- proj_weight: bfloat16 [4096, 4096], P('seq', 'tp'), may hold values from -0.09375 to 0.09375
- doc_ids: int32 [16384], P(('seq', 'tp')), may hold values from 0 to 63, never falling along the last dimension, each value on 1 to 1024 neighbouring positions
- stream_ids: int32 [16384], P(('seq', 'tp')), may hold values from 0 to 7
- stream_weight: float32 [8], replicated, may hold values from 0.25 to 4
Outputs:
- stream_loss: float32 [8], replicated
- w_grad: float32 [4096, 4096], P('seq', 'tp')
Inputs may be any that keep to these rules, and one draw needn't show every extreme that they name: `doc_ids`: never falls along the tokens; every document holds 1 to 1024 tokens, and one holds exactly 1024.
All inputs are finite; a program needn't handle non-finite values.
Results may differ from a plain program's by a relative error of at most 0.02.
Values may be sent and summed in bfloat16 or wider, within the bound.
A program may use at most 128 MiB of HBM per device.

v0:
```python
import jax
import jax.numpy as jnp
from jax import lax
from jax.sharding import PartitionSpec as P

DT = 16384
DOC_LEN = 256


EPS = 1e-05


def norm_rows(values, gain):
    floats = values.astype(jnp.float32)
    mean_sq = jnp.mean(floats * floats, axis=1, keepdims=True)
    return (floats * lax.rsqrt(mean_sq + EPS) * gain.astype(jnp.float32)[None, :]).astype(
        jnp.bfloat16
    )


def shards(
    teacher_hidden,
    teacher_gain,
    target_proj,
    student_in,
    student_gain,
    proj_weight,
    doc_ids,
    stream_ids,
    stream_weight,
):
    tp_count = lax.axis_size("tp")
    seq_count = lax.axis_size("seq")
    own_rows = student_in.shape[0]
    width_full = student_in.shape[1]
    doc_total = own_rows * tp_count * seq_count // DOC_LEN
    streams = stream_weight.shape[0]
    doc_range = jnp.arange(doc_total, dtype=jnp.int32)
    stream_range = jnp.arange(streams, dtype=jnp.int32)
    own_docs = (doc_ids[:, None] == doc_range[None, :]).astype(jnp.float32)
    doc_count = lax.psum(jnp.sum(own_docs, axis=0), ("seq", "tp"))
    teacher_float = teacher_hidden.astype(jnp.float32)
    square_sum = lax.psum(jnp.sum(teacher_float * teacher_float, axis=1), "tp")
    teacher_normed = (
        teacher_float
        * lax.rsqrt(square_sum / DT + EPS)[:, None]
        * teacher_gain.astype(jnp.float32)[None, :]
    ).astype(jnp.bfloat16)
    gathered = lax.all_gather(student_in, "tp", axis=0, tiled=True)
    normed = norm_rows(gathered, student_gain)
    inputs = normed
    hidden_cols = jnp.dot(
        inputs,
        lax.all_gather(proj_weight, "seq", axis=0, tiled=True),
        preferred_element_type=jnp.float32,
    ).astype(jnp.bfloat16)
    target = lax.psum_scatter(
        jnp.dot(teacher_normed, target_proj, preferred_element_type=jnp.float32).astype(
            jnp.bfloat16
        ),
        "tp",
        scatter_dimension=0,
        tiled=True,
    ).astype(jnp.float32)
    hidden_rows = lax.all_to_all(hidden_cols, "tp", split_axis=0, concat_axis=1, tiled=True)
    error = student_in.astype(jnp.float32) + hidden_rows.astype(jnp.float32) - target
    token_error = jnp.sum(error * error, axis=1) / width_full
    stream_table = (stream_ids[:, None] == stream_range[None, :]).astype(jnp.float32)
    doc_length = jnp.dot(own_docs, doc_count, precision=lax.Precision.HIGHEST)
    scale = 2.0 * jnp.dot(stream_table, stream_weight, precision=lax.Precision.HIGHEST) / doc_length
    grad_rows = (scale[:, None] * error).astype(jnp.bfloat16)
    grad_block = lax.all_to_all(grad_rows, "tp", split_axis=1, concat_axis=0, tiled=True)
    loss_terms = jnp.dot(
        own_docs.T, stream_table * token_error[:, None], precision=lax.Precision.HIGHEST
    )
    summed = lax.psum(loss_terms, ("seq", "tp"))
    stream_loss = jnp.sum(summed / doc_count[:, None], axis=0)
    inputs = normed
    w_grad = lax.psum_scatter(
        lax.dot_general(
            inputs, grad_block, (((0,), (0,)), ((), ())), preferred_element_type=jnp.float32
        ).astype(jnp.bfloat16),
        "seq",
        scatter_dimension=0,
        tiled=True,
    ).astype(jnp.float32)
    return (stream_loss, w_grad)


def solution(mesh):
    in_specs = (
        P("seq", "tp"),
        P("tp"),
        P("tp", None),
        P(("seq", "tp"), None),
        P(),
        P("seq", "tp"),
        P(("seq", "tp")),
        P(("seq", "tp")),
        P(),
    )
    out_specs = (P(), P("seq", "tp"))
    return jax.shard_map(shards, mesh=mesh, in_specs=in_specs, out_specs=out_specs, check_vma=False)
```

profile of v0, /device:TPU:0, one launch (start us, length us, event | category | flops | bytes accessed | tf_op | source)
XLA Modules:
  0.0 537.5 jit_solution(2509755592646255597)
XLA Ops:
  7.2 0.0 copy-start
  7.2 0.0 all-gather.3.cloned.1.call-start
  7.2 0.7 all-gather.3.cloned.1.call-update
  7.9 0.0 all-gather.5.cloned.1.call-start
  8.0 0.7 all-gather.5.cloned.1.call-update
  8.7 0.0 reduce-scatter.3.cloned.1.call-start
  8.7 0.7 convert_element_type.61
  9.4 3.1 fusion.3
  12.5 32.0 %psum.21 = f32[2048]{0:T(1024)S(1)} all-reduce(f32[2048]{0:T(1024)S(1)} %fusion.3), channel_id=1, replica_groups=mesh['seq'=8,'tp'=16] {'tp'}, use_global_device_ids=true, to_apply=%region_2.0 | all-reduce | flops 2048 | bytes 16384 | tf_op jit(solution)/shard_map/psum | solution.py:43
  44.5 25.0 %convolution_convert_fusion = bf16[2048,4096]{1,0:T(8,128)(2,1)} fusion(bf16[1024,4096]{1,0:T(8,128)(2,1)} %param.11, bf16[2048,1024]{1,0:T(8,128)(2,1)} %param.9, f32[1024]{0:T(1024)S(1)} %convert_element_type.61, f32[2048]{0:T(1024)S(1)} %add_rsqrt_fusion), kind=kOutput, calls=%fused_computation.5 | convolution fusion | flops 17196646400 | bytes 29372416 | tf_op jit(solution)/shard_map/dot_general | solution.py:58
  69.4 0.0 copy-start.2
  69.4 0.0 reduce-scatter.3.cloned.1.call-update
  69.5 0.7 copy-done.2
  70.1 34.3 %all-gather.3.cloned.1.call-done = bf16[2048,4096]{1,0:T(8,128)(2,1)} async-done(((bf16[128,4096]{1,0:T(8,128)(2,1)}), bf16[2048,4096]{1,0:T(8,128)(2,1)}) %all-gather.3.cloned.1.call-update) | async-done | bytes 16777232 | tf_op jit(solution)/shard_map/all_gather | solution.py:49
  104.4 7.2 %fusion = f32[2048]{0:T(1024)S(1)} fusion(bf16[2048,4096]{1,0:T(8,128)(2,1)} %all-gather.3.cloned.1.call-done), kind=kLoop, calls=%fused_computation.2 | loop fusion | flops 25163776 | bytes 16785408 | tf_op jit(solution)/shard_map/reduce_sum | solution.py:15
  111.7 0.0 copy-start.3
  111.7 50.3 %all-gather.5.cloned.1.call-done = bf16[4096,256]{1,0:T(8,128)(2,1)} async-done(((bf16[512,256]{1,0:T(8,128)(2,1)}), bf16[4096,256]{1,0:T(8,128)(2,1)}) %all-gather.5.cloned.1.call-update) | async-done | bytes 2097168 | tf_op jit(solution)/shard_map/all_gather | solution.py:54
  162.0 12.8 %fusion.12 = bf16[2048,256]{1,0:T(8,128)(2,1)} fusion(bf16[4096,256]{1,0:T(8,128)(2,1)} %all-gather.5.cloned.1.call-done, bf16[2048,4096]{1,0:T(8,128)(2,1)} %all-gather.3.cloned.1.call-done, f32[4096]{0:T(1024)S(1)} %convert_element_type.54, f32[2048]{0:T(1024)S(1)} %add_rsqrt_fusion.1), kind=kOutput, calls=%fused_computation.15 | convolution fusion | flops 4329046016 | bytes 19947520 | tf_op jit(solution)/shard_map/dot_general | solution.py:52
  174.8 0.0 copy-start.1
  174.8 0.0 copy-start.4
  174.8 4.5 all-to-all-start
  179.3 0.0 reduce-scatter.5.cloned.1.call-start
  179.4 0.0 copy-done.3
  179.4 0.1 convert_reduce_fusion
  179.5 27.9 %all-to-all-done = bf16[16,128,256]{2,1,0:T(8,128)(2,1)S(1)} async-done(((bf16[16,128,256]{2,1,0:T(8,128)(2,1)}), bf16[16,128,256]{2,1,0:T(8,128)(2,1)S(1)}, u32[]{:S(2)}, u32[]{:S(2)}) %all-to-all-start) | async-done | bytes 1048608 | tf_op jit(solution)/shard_map/all_to_all | solution.py:65
  207.4 0.2 convert_bitcast_fusion
  207.6 0.2 copy.17
  207.8 148.0 %reduce-scatter.3.cloned.1.call-done = bf16[128,4096]{1,0:T(8,128)(2,1)} async-done(((bf16[2048,4096]{1,0:T(8,128)(2,1)}), bf16[128,4096]{1,0:T(8,128)(2,1)}) %reduce-scatter.3.cloned.1.call-update) | async-done | bytes 1048592 | tf_op jit(solution)/shard_map/reduce_scatter | solution.py:57
  355.8 0.0 copy-done.1
  355.8 1.7 multiply_reduce_fusion
  357.5 0.0 copy-done.4
  357.5 0.3 fusion.17
  357.8 64.5 %all-reduce = (f32[64,8]{0,1:T(8,128)S(1)}, f32[64]{0:T(128)S(1)}) all-reduce(f32[64,8]{0,1:T(8,128)S(1)} %fusion.17, f32[64]{0:T(128)S(1)} %convert_reduce_fusion), channel_id=1, replica_groups=mesh['seq'=8,'tp'=16] {'seq','tp'}, use_global_device_ids=true, to_apply=%region_5.0 | all-reduce | flops 576 | bytes 4608 | tf_op jit(solution)/shard_map/psum | solution.py:76
  422.3 0.1 convolution_bitcast_fusion
  422.4 0.0 copy-done
  422.4 0.2 fusion.16
  422.6 1.8 multiply_convert_fusion
  424.4 0.1 copy.19
  424.5 19.4 %all_to_all.32 = bf16[128,16,256]{2,0,1:T(8,128)(2,1)S(1)} all-to-all(bf16[128,16,256]{2,0,1:T(8,128)(2,1)S(1)} %bitcast.31), channel_id=1, replica_groups=mesh['seq'=8,'tp'=16] {'tp'}, dimensions={1} | all-to-all | bytes 2097152 | tf_op jit(solution)/shard_map/all_to_all | solution.py:72
  443.9 13.6 %convolution_convert_fusion.1 = bf16[4096,256]{1,0:T(8,128)(2,1)} fusion(bf16[2048,256]{1,0:T(8,128)(2,1)S(1)} %bitcast.33, bf16[2048,4096]{1,0:T(8,128)(2,1)} %all-gather.3.cloned.1.call-done, f32[4096]{0:T(1024)S(1)} %convert_element_type.54, f32[2048]{0:T(1024)S(1)} %add_rsqrt_fusion.1), kind=kOutput, calls=%fused_computation.11 | convolution fusion | flops 4329570304 | bytes 19947520 | tf_op jit(solution)/shard_map/dot_general | solution.py:80
  457.5 0.0 reduce-scatter.5.cloned.1.call-update
  457.5 0.6 divide_reduce_fusion
  458.1 71.1 %reduce-scatter.5.cloned.1.call-done = bf16[512,256]{1,0:T(8,128)(2,1)} async-done(((bf16[4096,256]{1,0:T(8,128)(2,1)}), bf16[512,256]{1,0:T(8,128)(2,1)}) %reduce-scatter.5.cloned.1.call-update) | async-done | bytes 262160 | tf_op jit(solution)/shard_map/reduce_scatter | solution.py:79
  529.2 1.8 convert_element_type.68
  (4 shorter events, 0.0 us)
Async XLA Ops:
  7.2 415.2 %copy-start = (f32[8]{0:T(128)S(1)}, f32[8]{0:T(128)}, u32[]{:S(2)}) copy-start(f32[8]{0:T(128)} %param.17) | copy-start | bytes 100
  7.2 97.3 %all-gather.3.cloned.1.call-start = ((), (), s32[]{:S(2)}) async-start(), calls=%async_computation.4 | async-start | bytes 17825792 | tf_op jit(solution)/shard_map/all_gather | solution.py:49
  7.9 154.1 %all-gather.5.cloned.1.call-start = ((), (), s32[]{:S(2)}) async-start(), calls=%async_computation.5 | async-start | bytes 2359296 | tf_op jit(solution)/shard_map/all_gather | solution.py:54
  8.7 347.1 %reduce-scatter.3.cloned.1.call-start = ((), (), s32[]{:S(2)}) async-start(), calls=%async_computation.6 | async-start | bytes 17825792 | tf_op jit(solution)/shard_map/reduce_scatter | solution.py:57
  69.4 0.7 copy-start.2
  111.7 67.7 %copy-start.3 = (s32[128]{0:T(128)S(1)}, s32[128]{0:T(128)}, u32[]{:S(2)}) copy-start(s32[128]{0:T(128)} %param.15) | copy-start | bytes 1540
  174.8 181.0 %copy-start.1 = (bf16[128,4096]{1,0:T(8,128)(2,1)S(1)}, bf16[128,4096]{1,0:T(8,128)(2,1)}, u32[]{:S(2)}) copy-start(bf16[128,4096]{1,0:T(8,128)(2,1)} %param.12) | copy-start | bytes 3145732
  174.8 182.7 %copy-start.4 = (s32[128]{0:T(128)S(1)}, s32[128]{0:T(128)}, u32[]{:S(2)}) copy-start(s32[128]{0:T(128)} %param.16) | copy-start | bytes 1540
  174.8 32.6 %all-to-all-start = ((bf16[16,128,256]{2,1,0:T(8,128)(2,1)}), bf16[16,128,256]{2,1,0:T(8,128)(2,1)S(1)}, u32[]{:S(2)}, u32[]{:S(2)}) async-start(bf16[16,128,256]{2,1,0:T(8,128)(2,1)} %bitcast), calls=%async_computation | async-start | bytes 2097152 | tf_op jit(solution)/shard_map/all_to_all | solution.py:65
  179.3 349.9 %reduce-scatter.5.cloned.1.call-start = ((), (), s32[]{:S(2)}) async-start(), calls=%async_computation.7 | async-start | bytes 2359296 | tf_op jit(solution)/shard_map/reduce_scatter | solution.py:79
Sparse Core Ops, SparseCore 0:
  9.7 94.6 all-gather.2
  106.8 55.1 all-gather.4
  164.4 191.3 reduce-scatter.2
  457.6 71.5 reduce-scatter.4
where the time goes:
time: 538 us; the launch traced here: 537 us
  waiting for transfers between devices  333 us (62%)
  blocking collectives  116 us (22%)
  matrix products  51.9 us (10%)
  other arithmetic  17.2 us (3%)
  between operations  13.9 us (3%)
    reduce_scatter x1, waiting for transfers between devices, shards(): lax.psum_scatter(jnp.dot(teacher_normed, target_proj, preferred_element_t...  148 us
    reduce_scatter x1, waiting for transfers between devices, shards(): lax.psum_scatter(lax.dot_general(inputs, grad_block, (((0,), (0,)), ((),...  71.1 us
    psum x1, blocking collectives, shards(): summed = lax.psum(loss_terms, ('seq', 'tp'))  64.5 us
    all_gather x1, waiting for transfers between devices, shards(): lax.all_gather(proj_weight, 'seq', axis=0, tiled=True)  50.3 us
    all_gather x1, waiting for transfers between devices, shards(): gathered = lax.all_gather(student_in, 'tp', axis=0, tiled=True)  34.3 us
    psum x1, blocking collectives, shards(): square_sum = lax.psum(jnp.sum(teacher_float * teacher_float, axis=1), 'tp')  32 us
    all_to_all x1, waiting for transfers between devices, shards(): lax.all_to_all(hidden_cols, 'tp', split_axis=0, concat_axis=1, tiled=True)  27.9 us
    dot_general x1, matrix products, shards(): jnp.dot(teacher_normed, target_proj, preferred_element_type=jnp.float32)  25 us
  transfers between devices with their start and end apart: 5, of which 5 were waited for; matrix products, arithmetic and copies ran while one was open for 9% of the time, Pallas kernels for 0%

commit v1 on v0

v1 whole, which is shorter than its diff:
```python
import jax
import jax.numpy as jnp
from jax import lax
from jax.experimental import pallas as pl
from jax.experimental.pallas import tpu as pltpu
from jax.sharding import PartitionSpec as P

EPS = 1e-05
DT = 16384
D = 4096
NC = 4
SLOTS = 3
BF = jnp.bfloat16
F32 = jnp.float32
MESH = pl.DeviceIdType.MESH


def device(xh, z, y, xl, c):
    return {"seq": xh * 4 + z, "tp": (y * 2 + xl) * 2 + c}


def kernel(
    teacher,
    tgain,
    proj,
    student,
    sgain,
    weight,
    meta,
    wvec,
    out_t,
    out_loss,
    a_buf,
    b_buf,
    p_buf,
    r1_buf,
    r2_buf,
    sx_buf,
    rx_buf,
    nd_buf,
    w_buf,
    hs_buf,
    hr_buf,
    st_buf,
    gs_buf,
    gr_buf,
    gt_buf,
    dr1_buf,
    dr2_buf,
    ds_buf,
    dy_buf,
    fs_buf,
    fr_buf,
    m_buf,
    sq_buf,
    stat_buf,
    statr_buf,
    staty_buf,
    statz_buf,
    stato_buf,
    loss_buf,
    lossr_buf,
    rs_buf,
    sc_buf,
    ln_buf,
    te_buf,
    own_buf,
    send_sem,
    recv_sem,
    local_sem,
    cross_sem,
):
    s = lax.axis_index("seq")
    t = lax.axis_index("tp")
    xh, z = s // 4, s % 4
    y, xl, c = t // 4, (t // 2) % 2, t % 2
    x = xh * 2 + xl
    o = 1 - c

    def at_y(k):
        return device(xh, z, (y + k) % 4, xl, c)

    def at_z(k):
        return device(xh, (z + k) % 4, y, xl, c)

    def at_x(k):
        n = (x + k) % 4
        return device(n // 2, z, y, n % 2, c)

    sibling = device(xh, z, y, xl, o)
    x_pair = device(xh, z, y, 1 - xl, c)
    x_outer = device(1 - xh, z, y, 1 - xl, c)

    counts = {"s": 0, "r": 0, "l": 0}
    pending = []

    def local(src, dst):
        i = counts["l"]
        counts["l"] += 1
        cp = pltpu.make_async_copy(src, dst, local_sem.at[i])
        cp.start()
        return cp

    def remote(src, dst, to):
        i = counts["s"]
        counts["s"] += 1
        cp = pltpu.make_async_remote_copy(
            src_ref=src,
            dst_ref=dst,
            send_sem=send_sem.at[i],
            recv_sem=recv_sem.at[i],
            device_id=to,
            device_id_type=MESH,
        )
        cp.start()
        pending.append(cp)
        return cp

    def sent(cps):
        for cp in cps:
            cp.wait_send()
            pending[:] = [other for other in pending if other is not cp]

    def crossed(src, dst, to, itself, base):
        i = counts["s"]
        counts["s"] += 1
        cp = pltpu.make_async_remote_copy(
            src_ref=src,
            dst_ref=dst,
            send_sem=send_sem.at[i],
            recv_sem=cross_sem.at[base + xl],
            device_id=to,
            device_id_type=MESH,
        )
        own = pltpu.make_async_copy(src, dst, cross_sem.at[base + xl])

        @pl.when(itself)
        def _():
            own.start()

        @pl.when(jnp.logical_not(itself))
        def _():
            cp.start()

        return cp, itself

    def crossed_sent(pair):
        cp, itself = pair

        @pl.when(jnp.logical_not(itself))
        def _():
            cp.wait_send()

    st_load = local(student, st_buf.at[c])
    order = [2, 1, 3, 0]
    blocks = [((y + k) % 4) * 2 + h for k in order for h in range(2)]
    a_load = [local(teacher.at[b], a_buf.at[c, b]) for b in blocks]
    m_load = local(meta, m_buf.at[c])

    def proj_cols(j, yp, core):
        lane = yp * 1024 + (j // 2) * 512 + (j % 2) * 128 + core * 256
        return proj.at[:, :, pl.ds(pl.multiple_of(lane, 128), 128)]

    b_load = [
        [local(proj_cols(j, yp, c), b_buf.at[c, j, :, :, pl.ds(yp * 128, 128)]) for yp in range(4)]
        for j in range(NC)
    ]

    swapped = [device(xh, y, z, r, c) for r in range(2)]
    barrier = pltpu.get_barrier_semaphore()
    peers = [sibling, at_x(1), at_x(3)] + [at_y(k) for k in (1, 2, 3)] + [at_z(k) for k in (1, 2, 3)]
    for peer in peers:
        pl.semaphore_signal(barrier, inc=1, device_id=peer, device_id_type=MESH)

    @pl.when(y != z)
    def _():
        for peer in swapped:
            pl.semaphore_signal(barrier, inc=1, device_id=peer, device_id_type=MESH)
        pl.semaphore_wait(barrier, len(peers) + 2)

    @pl.when(y == z)
    def _():
        pl.semaphore_wait(barrier, len(peers))

    w_swap = [
        crossed(
            weight.at[pl.ds(r * 256, 256)],
            w_buf.at[xh * 2 + r, z, :, pl.ds(pl.multiple_of(xl * 256, 128), 256)],
            swapped[r],
            jnp.logical_and(y == z, xl == r),
            0,
        )
        for r in range(2)
    ]

    def send_b(j):
        return [
            remote(proj_cols(j, yp, o), b_buf.at[c, j, :, :, pl.ds(yp * 128, 128)], sibling)
            for yp in range(4)
        ]

    b_recv = [send_b(0)]

    st_load.wait()
    sgain_f = sgain[...].astype(F32)

    def norm_rows(i, _):
        rows = pl.ds(pl.multiple_of(i * 16, 16), 16)
        v = st_buf[c, rows, :].astype(F32)
        scale = lax.rsqrt(jnp.sum(v * v, axis=1, keepdims=True) / D + EPS)
        n = (v * scale * sgain_f).astype(BF)
        for p in range(4):
            for zp in range(4):
                src = (p // 2) * 2048 + zp * 512 + (p % 2) * 256
                nd_buf[z, c, rows, pl.ds(p * 1024 + zp * 256, 256)] = n[:, src : src + 256]
        return 0

    lax.fori_loop(0, 8, norm_rows, 0)

    def half(h):
        return pl.ds(h * 64, 64)

    nd_right, nd_left = [None, None], [None, None]
    for first in range(2):
        h = first
        nd_right[h] = remote(nd_buf.at[z, c, half(h)], nd_buf.at[z, c, half(h)], at_z(1))
        h = 1 - first
        nd_left[h] = remote(nd_buf.at[z, c, half(h)], nd_buf.at[z, c, half(h)], at_z(3))

    tgain_f = tgain[...].astype(F32)
    ones = jnp.ones((8, 1024), BF)
    a_recv = []
    for load, b in zip(a_load, blocks):
        load.wait()

        def prep(r, _, b=b):
            rows = pl.ds(pl.multiple_of(r * 128, 128), 128)
            v = a_buf[c, b, rows, :].astype(F32)
            squares = (v * v).astype(BF)
            sq_buf[b * 2 + r] = lax.dot_general(
                ones, squares, (((1,), (1,)), ((), ())), preferred_element_type=F32
            )
            a_buf[c, b, rows, :] = (v * tgain_f).astype(BF)
            return 0

        lax.fori_loop(0, 2, prep, 0)
        a_recv.append(remote(a_buf.at[c, b], a_buf.at[c, b], sibling))

    st_recv = remote(st_buf.at[c], st_buf.at[c], sibling)
    m_load.wait()
    m_recv = remote(m_buf.at[c], m_buf.at[c], sibling)
    nd_side = [remote(nd_buf.at[z, c], nd_buf.at[z, c], sibling)]
    for j in range(1, NC):
        b_recv.append(send_b(j))

    for n in range(2):
        got = w_buf.at[x, y, :, pl.ds(n * 256, 256)]
        pltpu.make_async_copy(got, got, cross_sem.at[n]).wait()

    def cols(h):
        return pl.ds(h * 256, 256)

    w_y = [
        [remote(w_buf.at[x, y, :, cols(h)], w_buf.at[x, y, :, cols(h)], at_y(k)) for k in (1, 2, 3)]
        for h in range(2)
    ]

    for i in range(16):
        stat_buf[0, i : i + 1, :] = sq_buf[i, 0:1, :]
    own_counts = jnp.sum(m_buf[c], axis=0, keepdims=True)
    stat_buf[0, 16:24, :] = jnp.broadcast_to(own_counts, (8, 128))

    stat_c = remote(stat_buf.at[0], statr_buf.at[0], sibling)

    def block_out(j, k):
        slot = j % SLOTS

        def body(h, _):
            b = ((y + k) % 4) * 2 + h
            acc = jnp.dot(
                a_buf[0, b], b_buf[0, j].reshape(1024, 512), preferred_element_type=F32
            )
            acc = acc + jnp.dot(
                a_buf[1, b], b_buf[1, j].reshape(1024, 512), preferred_element_type=F32
            )
            p_buf[slot, b] = acc.astype(BF)
            return 0

        lax.fori_loop(0, 2, body, 0)

    r1 = [None] * NC
    r2 = [None] * NC
    p_sends = [None] * NC

    def part(k, h):
        return ((y + k) % 4) * 2 + h

    def stage_a(j):
        slot = j % SLOTS
        if j >= SLOTS:
            sent(p_sends[j - SLOTS])
        for cp in b_load[j]:
            cp.wait()
        for cp in b_recv[j]:
            cp.wait_recv()
        for n, k in enumerate(order):
            if j == 0:
                a_recv[2 * n].wait_recv()
                a_recv[2 * n + 1].wait_recv()
            block_out(j, k)
            if k == 2:
                r1[j] = [
                    remote(p_buf.at[slot, part(2, 0)], r1_buf.at[j, 0], at_y(1)),
                    remote(p_buf.at[slot, part(2, 1)], r1_buf.at[j, 1], at_y(3)),
                ]
            elif k == 1:
                right = remote(p_buf.at[slot, part(1, 1)], r2_buf.at[j, 0, 1], at_y(1))
            elif k == 3:
                left = remote(p_buf.at[slot, part(3, 0)], r2_buf.at[j, 1, 0], at_y(3))
        r2[j] = [right, left]
        p_sends[j] = r1[j] + [right, left]

    def stage_b(j):
        slot = j % SLOTS
        for i, (k, h) in enumerate(((1, 0), (3, 1))):
            r1[j][i].wait_recv()
            b = part(k, h)
            p_buf[slot, b] = (p_buf[slot, b].astype(F32) + r1_buf[j, i].astype(F32)).astype(BF)
            cp = remote(p_buf.at[slot, b], r2_buf.at[j, i, h], at_y(k))
            r2[j].append(cp)
            p_sends[j].append(cp)

    def summed(j, h, lanes):
        slot = j % SLOTS
        return (
            p_buf[slot, part(0, h), :, lanes].astype(F32)
            + r2_buf[j, 0, h, :, lanes].astype(F32)
            + r2_buf[j, 1, h, :, lanes].astype(F32)
        )

    rx = [None] * NC

    def stage_c(j):
        for cp in r2[j]:
            cp.wait_recv()
        for i in range(4):
            lanes = pl.ds(i * 128, 128)
            sx_buf[j, :, lanes] = summed(j, 1 - xl, lanes).astype(BF)
            own_buf[j % 2, :, lanes] = summed(j, xl, lanes)
        rx[j] = remote(sx_buf.at[j], rx_buf.at[j], x_pair)

    gr = [None] * NC

    def stage_d(j):
        rx[j].wait_recv()
        for yp in range(4):
            lanes = pl.ds(yp * 128, 128)
            target = own_buf[j % 2, :, lanes] + rx_buf[j, :, lanes].astype(F32)
            lane = yp * 1024 + (j // 2) * 512 + (j % 2) * 128 + c * 256
            st = st_buf[:, :, pl.ds(pl.multiple_of(lane, 128), 128)].reshape(256, 128)
            hidden = hr_buf[yp, :, pl.ds(j * 128, 128)]
            error = st.astype(F32) + hidden.astype(F32) - target * rs_buf[...]
            if j == 0 and yp == 0:
                te_buf[...] = error * error
            else:
                te_buf[...] += error * error
            gs_buf[j, yp] = (error * sc_buf[...]).astype(BF)
        gr[j] = [
            remote(gs_buf.at[j, (z + k) % 4], gr_buf.at[j, z], at_z(k)) for k in (2, 1, 3)
        ]
        gr_buf[j, z] = gs_buf[j, z]

    d1 = [None] * NC
    d2 = [None] * NC

    def dpart(k, h):
        return ((x + k) % 4) * 2 + h

    def stage_e(j):
        for cp in gr[j]:
            cp.wait_recv()
        gt_buf[...] = gr_buf[j].reshape(1024, 128).T
        for k in order:

            def body(h, _, k=k):
                b = dpart(k, h)
                lanes = pl.ds(pl.multiple_of(b * 512, 512), 512)
                nd = nd_buf[:, :, :, lanes].reshape(1024, 512)
                b_buf[0, j, b] = jnp.dot(gt_buf[...], nd, preferred_element_type=F32).astype(BF)
                return 0

            lax.fori_loop(0, 2, body, 0)
            if k == 2:
                d1[j] = [
                    remote(b_buf.at[0, j, dpart(2, 0)], dr1_buf.at[j, 0], at_x(1)),
                    remote(b_buf.at[0, j, dpart(2, 1)], dr1_buf.at[j, 1], at_x(3)),
                ]
            elif k == 1:
                right = remote(b_buf.at[0, j, dpart(1, 1)], dr2_buf.at[j, 0, 1], at_x(1))
            elif k == 3:
                left = remote(b_buf.at[0, j, dpart(3, 0)], dr2_buf.at[j, 1, 0], at_x(3))
        d2[j] = [right, left]

    def stage_f(j):
        for i, (k, h) in enumerate(((1, 0), (3, 1))):
            d1[j][i].wait_recv()
            b = dpart(k, h)
            b_buf[0, j, b] = (b_buf[0, j, b].astype(F32) + dr1_buf[j, i].astype(F32)).astype(BF)
            d2[j].append(remote(b_buf.at[0, j, b], dr2_buf.at[j, i, h], at_x(k)))

    dy = [None] * NC

    def stage_g(j):
        for cp in d2[j]:
            cp.wait_recv()
        for zp in range(4):
            h, lanes = zp // 2, pl.ds((zp % 2) * 256, 256)
            ds_buf[j, zp] = (
                b_buf[0, j, dpart(0, h), :, lanes].astype(F32)
                + dr2_buf[j, 0, h, :, lanes].astype(F32)
                + dr2_buf[j, 1, h, :, lanes].astype(F32)
            ).astype(BF)
        dy[j] = [
            remote(ds_buf.at[j, (y + k) % 4], dy_buf.at[j, y], at_y(k)) for k in (2, 1, 3)
        ]

    final = [None] * NC

    def stage_h(j):
        for cp in dy[j]:
            cp.wait_recv()
        total = ds_buf[j, y].astype(F32)
        for k in (1, 2, 3):
            total = total + dy_buf[j, (y + k) % 4].astype(F32)
        fs_buf[j] = total.astype(BF)
        final[j] = crossed(
            fs_buf.at[j],
            fr_buf.at[j % 2, xl],
            device(xh, y, z, j // 2, c),
            jnp.logical_and(y == z, xl == j // 2),
            2 + 2 * (j % 2),
        )

    w_x = [None, None]

    def gather_x1(h):
        for cp in w_y[h]:
            cp.wait_recv()
        w_x[h] = [remote(w_buf.at[x, :, :, cols(h)], w_buf.at[x, :, :, cols(h)], at_x(k)) for k in (1, 3)]

    w_f = [None, None]

    def gather_x2(h):
        w_x[h][0].wait_recv()
        left = w_buf.at[(x + 3) % 4, pl.ds(0, 2), :, cols(h)]
        a = remote(left, left, at_x(1))
        w_x[h][1].wait_recv()
        right = w_buf.at[(x + 1) % 4, pl.ds(2, 2), :, cols(h)]
        w_f[h] = [a, remote(right, right, at_x(3))]

    stage_a(0)
    stat_c.wait_recv()
    stat_buf[1] = stat_buf[0] + statr_buf[0]
    stat_x = remote(stat_buf.at[1], statr_buf.at[1], x_pair)
    gather_x1(0)
    stage_a(1)

    nd_right[0].wait_recv()
    from_left = nd_buf.at[(z + 3) % 4, c, half(0)]
    nd_f0 = remote(from_left, from_left, at_z(1))
    nd_left[1].wait_recv()
    from_right = nd_buf.at[(z + 1) % 4, c, half(1)]
    nd_f1 = remote(from_right, from_right, at_z(3))
    gather_x1(1)
    stat_x.wait_recv()
    stat_buf[2] = stat_buf[1] + statr_buf[1]
    stat_y = [remote(stat_buf.at[2], staty_buf.at[y], at_y(k)) for k in (1, 2, 3)]
    staty_buf[y] = stat_buf[2]

    stage_b(0)
    stage_a(2)
    gather_x2(0)
    for cp in stat_y:
        cp.wait_recv()
    stat = staty_buf[0] + staty_buf[1] + staty_buf[2] + staty_buf[3]
    stat_buf[3] = stat
    statz_buf[z] = stat[16:24]
    stat_z = [remote(stat_buf.at[3, pl.ds(16, 8)], statz_buf.at[z], at_z(k)) for k in (1, 2, 3)]
    nd_right[1].wait_recv()
    nd_left[0].wait_recv()
    for k in (1, 3):
        whole = nd_buf.at[(z + k) % 4, c]
        nd_side.append(remote(whole, whole, sibling))
    stage_b(1)
    gather_x2(1)
    for cp in stat_z:
        cp.wait_recv()
    stato_buf[0] = statz_buf[0] + statz_buf[1] + statz_buf[2] + statz_buf[3]
    stat_o = remote(stato_buf.at[0], stato_buf.at[1], x_outer)
    nd_f0.wait_recv()
    nd_f1.wait_recv()
    whole = nd_buf.at[(z + 2) % 4, c]
    nd_side.append(remote(whole, whole, sibling))
    stage_c(0)
    stage_a(3)

    stat_o.wait_recv()
    m_recv.wait_recv()
    lanes_i = lax.broadcasted_iota(jnp.int32, (8, 128), 1)
    doc_counts = jnp.where(lanes_i < 64, stato_buf[0] + stato_buf[1], 0.0)[0:1]
    stream_w = wvec[0:1]
    rows_i = lax.broadcasted_iota(jnp.int32, (24, 128), 0)
    eye = lax.broadcasted_iota(jnp.int32, (128, 128), 0) == lax.broadcasted_iota(
        jnp.int32, (128, 128), 1
    )
    for core in range(2):
        rows = pl.ds(core * 128, 128)
        row = jnp.sum(
            jnp.where(rows_i == (y * 2 + xl) * 2 + core, stat_buf[3], 0.0), axis=0, keepdims=True
        )
        col = jnp.sum(
            jnp.where(eye, jnp.broadcast_to(row, (128, 128)), 0.0), axis=1, keepdims=True
        )
        rs_buf[rows] = jnp.broadcast_to(lax.rsqrt(col / DT + EPS), (128, 128))
        m = m_buf[core]
        length = jnp.sum(m * doc_counts, axis=1, keepdims=True)
        sw = jnp.sum(m * stream_w, axis=1, keepdims=True)
        sc_buf[rows] = jnp.broadcast_to(2.0 * sw / length, (128, 128))
        ln_buf[rows] = jnp.broadcast_to(length, (128, 128))
    st_recv.wait_recv()

    for cp in nd_side:
        cp.wait_recv()
    for h in range(2):
        for cp in w_f[h]:
            cp.wait_recv()
    hr = []
    for k in order:
        zd = (z + k) % 4
        hs_buf[zd] = jnp.dot(
            nd_buf[zd].reshape(256, D), w_buf[...].reshape(D, 512), preferred_element_type=F32
        ).astype(BF)
        if k:
            hr.append(remote(hs_buf.at[zd], hr_buf.at[z], at_z(k)))
    hr_buf[z] = hs_buf[z]

    stage_b(2)
    stage_c(1)
    for cp in hr:
        cp.wait_recv()
    stage_d(0)
    stage_d(1)
    stage_b(3)
    stage_e(0)
    stage_c(2)
    stage_f(0)
    stage_e(1)
    stage_d(2)
    stage_g(0)
    stage_f(1)
    stage_e(2)
    stage_h(0)
    stage_c(3)
    stage_g(1)
    stage_f(2)
    stage_d(3)

    def loss_of(core):
        rows = pl.ds(core * 128, 128)
        te = jnp.sum(te_buf[rows], axis=1, keepdims=True) / D
        return jnp.sum(m_buf[core] * (te / ln_buf[rows]), axis=0, keepdims=True)

    loss_buf[0] = jnp.broadcast_to(loss_of(0) + loss_of(1), (8, 128))
    loss_c = remote(loss_buf.at[0], lossr_buf.at[0], sibling)
    stage_h(1)
    stage_e(3)
    loss_c.wait_recv()
    loss_buf[1] = loss_buf[0] + lossr_buf[0]
    loss_x = remote(loss_buf.at[1], lossr_buf.at[1], x_pair)
    stage_g(2)
    stage_f(3)
    loss_x.wait_recv()
    loss_buf[2] = loss_buf[1] + lossr_buf[1]
    lossr_buf[4 + y] = loss_buf[2]
    loss_y = [remote(loss_buf.at[2], lossr_buf.at[4 + y], at_y(k)) for k in (1, 2, 3)]
    stage_h(2)
    for cp in loss_y:
        cp.wait_recv()
    loss_buf[3] = lossr_buf[4] + lossr_buf[5] + lossr_buf[6] + lossr_buf[7]
    lossr_buf[8 + z] = loss_buf[3]
    loss_z = [remote(loss_buf.at[3], lossr_buf.at[8 + z], at_z(k)) for k in (1, 2, 3)]
    stage_g(3)
    for cp in loss_z:
        cp.wait_recv()
    loss_buf[4] = lossr_buf[8] + lossr_buf[9] + lossr_buf[10] + lossr_buf[11]
    loss_o = remote(loss_buf.at[4], lossr_buf.at[2], x_outer)
    stage_h(3)
    loss_o.wait_recv()
    out_loss[...] = loss_buf[4] + lossr_buf[2]

    for jj in range(2):
        for r in range(2):
            got = fr_buf.at[jj, r]
            pltpu.make_async_copy(got, got, cross_sem.at[2 + 2 * jj + r]).wait()
    for pair in w_swap + final:
        crossed_sent(pair)
    for jj in range(2):
        for r in range(2):
            out_t[pl.ds(jj * 128, 128), pl.ds(r * 256, 256)] = fr_buf[jj, r]
    for cp in list(pending):
        cp.wait_send()


def shards(
    teacher_hidden,
    teacher_gain,
    target_proj,
    student_in,
    student_gain,
    proj_weight,
    doc_ids,
    stream_ids,
    stream_weight,
):
    lane = jnp.arange(128, dtype=jnp.int32)[None, :]
    meta = jnp.where(
        lane < 64, doc_ids[:, None] == lane, stream_ids[:, None] == lane - 64
    ).astype(F32)
    wvec = jnp.broadcast_to(jnp.pad(stream_weight, (64, 56))[None, :], (8, 128))
    hbm = pl.BlockSpec(memory_space=pl.ANY)
    vmem = pl.BlockSpec(memory_space=pltpu.VMEM)
    scratch = [
        ((2, 8, 256, 1024), BF),
        ((2, NC, 8, 128, 512), BF),
        ((SLOTS, 8, 256, 512), BF),
        ((NC, 2, 256, 512), BF),
        ((NC, 2, 2, 256, 512), BF),
        ((NC, 256, 512), BF),
        ((NC, 256, 512), BF),
        ((4, 2, 128, D), BF),
        ((4, 4, 256, 512), BF),
        ((4, 256, 512), BF),
        ((4, 256, 512), BF),
        ((2, 128, D), BF),
        ((NC, 4, 256, 128), BF),
        ((NC, 4, 256, 128), BF),
        ((128, 1024), BF),
        ((NC, 2, 128, 512), BF),
        ((NC, 2, 2, 128, 512), BF),
        ((NC, 4, 128, 256), BF),
        ((NC, 4, 128, 256), BF),
        ((NC, 128, 256), BF),
        ((2, 2, 128, 256), BF),
        ((2, 128, 128), F32),
        ((16, 8, 128), F32),
        ((4, 24, 128), F32),
        ((2, 24, 128), F32),
        ((4, 24, 128), F32),
        ((4, 8, 128), F32),
        ((2, 8, 128), F32),
        ((5, 8, 128), F32),
        ((12, 8, 128), F32),
        ((256, 128), F32),
        ((256, 128), F32),
        ((256, 128), F32),
        ((256, 128), F32),
        ((2, 256, 512), F32),
    ]
    out_t, loss = pl.pallas_call(
        kernel,
        out_shape=(
            jax.ShapeDtypeStruct((256, 512), BF),
            jax.ShapeDtypeStruct((8, 128), F32),
        ),
        in_specs=[hbm, vmem, hbm, hbm, vmem, hbm, hbm, vmem],
        out_specs=(vmem, vmem),
        scratch_shapes=[pltpu.VMEM(shape, kind) for shape, kind in scratch]
        + [
            pltpu.SemaphoreType.DMA((224,)),
            pltpu.SemaphoreType.DMA((224,)),
            pltpu.SemaphoreType.DMA((32,)),
            pltpu.SemaphoreType.DMA((6,)),
        ],
        compiler_params=pltpu.CompilerParams(
            collective_id=0, has_side_effects=True, vmem_limit_bytes=62 * 2**20
        ),
        cost_estimate=pl.CostEstimate(flops=26 * 10**9, bytes_accessed=16 * 2**20, transcendentals=0),
    )(
        teacher_hidden.reshape(8, 256, 1024),
        teacher_gain.reshape(1, 1024),
        target_proj.reshape(8, 128, D),
        student_in,
        student_gain.reshape(1, D),
        proj_weight,
        meta,
        wvec,
    )
    return loss[0, 64:72], out_t.T.astype(F32)


def solution(mesh):
    in_specs = (
        P("seq", "tp"),
        P("tp"),
        P("tp", None),
        P(("seq", "tp"), None),
        P(),
        P("seq", "tp"),
        P(("seq", "tp")),
        P(("seq", "tp")),
        P(),
    )
    out_specs = (P(), P("seq", "tp"))
    return jax.shard_map(shards, mesh=mesh, in_specs=in_specs, out_specs=out_specs, check_vma=False)
```

time: 538 us -> 169 us (0.31)
  waiting for transfers between devices: 333 us -> 0 us
  Pallas kernels: 0 us -> 158 us
  blocking collectives: 116 us -> 0 us
  matrix products: 51.9 us -> 0 us
  other arithmetic: 17.2 us -> 2.41 us
  between operations: 13.9 us -> 0.65 us
    reduce_scatter x2 -> x0, waiting for transfers between devices: 219 us -> none  [the longest x1 148 us: shards(): lax.psum_scatter(jnp.dot(teacher_normed, target_proj, preferred_element_t...]
    pallas_call x0 -> x1, Pallas kernels: none -> 158 us  [shards(): pl.pallas_call(kernel, out_shape=(jax.ShapeDtypeStruct((256, 512), BF), j...]
    psum x2 -> x0, blocking collectives: 96.4 us -> none  [the longest x1 64.5 us: shards(): summed = lax.psum(loss_terms, ('seq', 'tp'))]
    all_gather x2 -> x0, waiting for transfers between devices: 84.6 us -> none  [the longest x1 50.3 us: shards(): lax.all_gather(proj_weight, 'seq', axis=0, tiled=True)]
    dot_general x6 -> x0, matrix products: 51.9 us -> none  [the longest x1 25 us: shards(): jnp.dot(teacher_normed, target_proj, preferred_element_type=jnp.float32)]
    all_to_all x1 -> x0, waiting for transfers between devices: 27.9 us -> none  [shards(): lax.all_to_all(hidden_cols, 'tp', split_axis=0, concat_axis=1, tiled=True)]
    all_to_all x1 -> x0, blocking collectives: 19.4 us -> none  [shards(): lax.all_to_all(grad_rows, 'tp', split_axis=1, concat_axis=0, tiled=True)]
    reduce_sum x5 -> x0, other arithmetic: 12.8 us -> none  [the longest x1 7.2 us: norm_rows(): mean_sq = jnp.mean(floats * floats, axis=1, keepdims=True)]
  transfers between devices with their start and end apart: 5 -> 0, of which waited for: 5 -> 0; matrix products, arithmetic and copies ran while one was open for 9% -> 0% of each run, Pallas kernels for 0% -> 0%
where the time goes in v1:
time: 169 us; the launch traced here: 168 us
  Pallas kernels  158 us (93%)
  local copies, waits for them, and re-layouts  6.16 us (4%)
  other arithmetic  2.41 us (1%)
    pallas_call x1, Pallas kernels, shards(): pl.pallas_call(kernel, out_shape=(jax.ShapeDtypeStruct((256, 512), BF), j...  158 us

profile of v1, /device:TPU:0, one launch (start us, length us, event | category | flops | bytes accessed | tf_op | source)
XLA Modules:
  0.0 167.5 jit_solution(380858273105798592)
XLA Ops:
  0.6 0.7 pad.4
  1.4 0.6 broadcast_in_dim.11.wvec
  2.0 1.3 reshape.30.tgain
  3.2 1.3 reshape.32.sgain
  4.5 1.4 fusion.1.meta
  5.9 158.3 %shard_map.104 = (bf16[256,512]{1,0:T(8,128)(2,1)}, f32[8,128]{1,0:T(8,128)}) custom-call(bf16[8,256,1024]{2,1,0:T(8,128)(2,1)} %bitcast.7, bf16[1,1024]{1,0:T(2,128)(2,1)} %reshape.30.tgain, bf16[8,128,4096]{2,1,0:T(8,128)(2,1)} %bitcast.6, bf16[128,4096]{1,0:T(8,128)(2,1)} %student.1, bf16[1,4096]{1,0:T(2,128)(2,1)} %reshape.32.sgain, ...), custom_call_target="tpu_custom_call" | custom-call | flops 25999998976 | bytes 16777216 | tf_op jit(solution)/shard_map/pallas_call | solution.py:669
  164.2 1.3 slice_bitcast_fusion
  165.5 1.0 convert_bitcast_fusion
  166.5 1.0 copy.11
  (2 shorter events, 0.0 us)

commit v2 on v1

v2 whole, which is shorter than its diff:
```python
import jax
import jax.numpy as jnp
from jax import lax
from jax.experimental import pallas as pl
from jax.experimental.pallas import tpu as pltpu
from jax.sharding import PartitionSpec as P

EPS = 1e-05
DT = 16384
D = 4096
NC = 4
SEMS = 160
SLOTS = 3
BF = jnp.bfloat16
F32 = jnp.float32
MESH = pl.DeviceIdType.MESH


def device(xh, z, y, xl, c):
    return {"seq": xh * 4 + z, "tp": (y * 2 + xl) * 2 + c}


def kernel(
    teacher,
    tgain,
    proj,
    student,
    sgain,
    weight,
    docs,
    streams,
    wstream,
    out_grad,
    out_loss,
    a_buf,
    b_buf,
    p_buf,
    r1_buf,
    r2_buf,
    sx_buf,
    rx_buf,
    nd_buf,
    w_buf,
    hs_buf,
    hr_buf,
    st_buf,
    gs_buf,
    gr_buf,
    gt_buf,
    dr1_buf,
    dr2_buf,
    ds_buf,
    dy_buf,
    fs_buf,
    fr_buf,
    m_buf,
    sq_buf,
    stat_buf,
    statr_buf,
    staty_buf,
    statz_buf,
    stato_buf,
    loss_buf,
    lossr_buf,
    rs_buf,
    sc_buf,
    ln_buf,
    te_buf,
    own_buf,
    sem,
    cross_sem,
):
    s = lax.axis_index("seq")
    t = lax.axis_index("tp")
    xh, z = s // 4, s % 4
    y, xl, c = t // 4, (t // 2) % 2, t % 2
    x = xh * 2 + xl
    o = 1 - c

    def at_y(k):
        return device(xh, z, (y + k) % 4, xl, c)

    def at_z(k):
        return device(xh, (z + k) % 4, y, xl, c)

    def at_x(k):
        n = (x + k) % 4
        return device(n // 2, z, y, n % 2, c)

    sibling = device(xh, z, y, xl, o)
    x_pair = device(xh, z, y, 1 - xl, c)
    x_outer = device(1 - xh, z, y, 1 - xl, c)

    used = [0]
    open_sends = []

    def new_sem():
        used[0] += 1
        return sem.at[used[0] - 1]

    class Group:
        def __init__(self, cover):
            self.cover, self.out, self.got = cover, new_sem(), new_sem()
            open_sends.append(self)

        def send(self, src, dst, to):
            pltpu.make_async_remote_copy(
                src_ref=src,
                dst_ref=dst,
                send_sem=self.out,
                recv_sem=self.got,
                device_id=to,
                device_id_type=MESH,
            ).start()
            return self

        def wait_recv(self):
            pltpu.make_async_copy(self.cover, self.cover, self.got).wait()

        def wait_send(self):
            pltpu.make_async_copy(self.cover, self.cover, self.out).wait()
            open_sends[:] = [other for other in open_sends if other is not self]

    def remote(src, dst, to):
        return Group(src).send(src, dst, to)

    class Load:
        def __init__(self, cover, pairs):
            self.cover, self.sem = cover, new_sem()
            for src, dst in pairs:
                pltpu.make_async_copy(src, dst, self.sem).start()

        def wait(self):
            pltpu.make_async_copy(self.cover, self.cover, self.sem).wait()

    def crossed(src, dst, to, itself, base):
        out = new_sem()
        cp = pltpu.make_async_remote_copy(
            src_ref=src,
            dst_ref=dst,
            send_sem=out,
            recv_sem=cross_sem.at[base + xl],
            device_id=to,
            device_id_type=MESH,
        )
        own = pltpu.make_async_copy(src, dst, cross_sem.at[base + xl])

        @pl.when(itself)
        def _():
            own.start()

        @pl.when(jnp.logical_not(itself))
        def _():
            cp.start()

        return cp, itself

    def crossed_sent(pair):
        cp, itself = pair

        @pl.when(jnp.logical_not(itself))
        def _():
            cp.wait_send()

    takers = [(k, r, device(xh, y, k, r, c)) for k in range(4) for r in range(2)]
    givers = [(k, r, device(xh, k, z, r, c)) for k in range(4) for r in range(2)]
    barrier = pltpu.get_barrier_semaphore()
    peers = [sibling, at_x(1), at_x(3)] + [at_y(k) for k in (1, 2, 3)] + [at_z(k) for k in (1, 2, 3)]
    for peer in peers:
        pl.semaphore_signal(barrier, inc=1, device_id=peer, device_id_type=MESH)

    for k, r, peer in givers:

        @pl.when(jnp.logical_not(jnp.logical_and(y == z, jnp.logical_and(k == z, r == xl))))
        def _(peer=peer):
            pl.semaphore_signal(barrier, inc=1, device_id=peer, device_id_type=MESH)

    st_load = Load(st_buf.at[c], [(student, st_buf.at[c])])
    order = [2, 3, 0, 1]

    def pair_of(core, k):
        return a_buf.at[core, pl.ds(((y + k) % 4) * 2, 2)]

    a_load = [
        Load(pair_of(c, k), [(teacher.at[pl.ds(((y + k) % 4) * 2, 2)], pair_of(c, k))]) for k in order
    ]

    def proj_cols(j, yp, core):
        lane = yp * 1024 + (j // 2) * 512 + (j % 2) * 128 + core * 256
        return proj.at[:, :, pl.ds(pl.multiple_of(lane, 128), 128)]

    b_load = [
        Load(
            b_buf.at[c, j],
            [(proj_cols(j, yp, c), b_buf.at[c, j, :, :, pl.ds(yp * 128, 128)]) for yp in range(4)],
        )
        for j in range(NC)
    ]

    sgain_f = sgain[...].astype(F32)
    sgain_f = jnp.concatenate([sgain_f[i : i + 1] for i in range(D // 128)], axis=1)
    st_load.wait()

    def norm_rows(i, _):
        rows = pl.ds(pl.multiple_of(i * 16, 16), 16)
        v = st_buf[c, rows, :].astype(F32)
        scale = lax.rsqrt(jnp.sum(v * v, axis=1, keepdims=True) / D + EPS)
        n = (v * scale * sgain_f).astype(BF)
        for p in range(4):
            for zp in range(4):
                src = (p // 2) * 2048 + zp * 512 + (p % 2) * 256
                nd_buf[z, c, rows, pl.ds(p * 1024 + zp * 256, 256)] = n[:, src : src + 256]
        return 0

    lax.fori_loop(0, 8, norm_rows, 0)

    @pl.when(y != z)
    def _():
        pl.semaphore_wait(barrier, len(peers) + 8)

    @pl.when(y == z)
    def _():
        pl.semaphore_wait(barrier, len(peers) + 7)

    w_swap = [
        crossed(
            weight.at[pl.ds(r * 256, 256)],
            w_buf.at[xh * 2 + r, z, :, pl.ds(pl.multiple_of(xl * 256, 128), 256)],
            peer,
            jnp.logical_and(y == z, jnp.logical_and(k == y, r == xl)),
            0,
        )
        for k, r, peer in takers
    ]

    def send_b(j):
        g = Group(b_buf.at[c, j])
        for yp in range(4):
            g.send(proj_cols(j, yp, o), b_buf.at[c, j, :, :, pl.ds(yp * 128, 128)], sibling)
        return g

    b_recv = [send_b(0)]

    def half(h):
        return pl.ds(h * 64, 64)

    nd_right, nd_left = [None, None], [None, None]
    for first in range(2):
        own = nd_buf.at[z, c, half(first)]
        nd_right[first] = remote(own, own, at_z(1))
        own = nd_buf.at[z, c, half(1 - first)]
        nd_left[1 - first] = remote(own, own, at_z(3))

    tgain_f = tgain[...].astype(F32)
    tgain_f = jnp.concatenate([tgain_f[i : i + 1] for i in range(8)], axis=1)
    ones = jnp.ones((8, 1024), BF)
    a_recv = []
    for load, k in zip(a_load, order):
        load.wait()

        def prep(r, _, k=k):
            b = ((y + k) % 4) * 2 + r // 2
            rows = pl.ds(pl.multiple_of((r % 2) * 128, 128), 128)
            v = a_buf[c, b, rows, :].astype(F32)
            squares = (v * v).astype(BF)
            sq_buf[((y + k) % 4) * 4 + r] = lax.dot_general(
                ones, squares, (((1,), (1,)), ((), ())), preferred_element_type=F32
            )
            a_buf[c, b, rows, :] = (v * tgain_f).astype(BF)
            return 0

        lax.fori_loop(0, 4, prep, 0)
        a_recv.append(remote(pair_of(c, k), pair_of(c, k), sibling))

    eye = lax.broadcasted_iota(jnp.int32, (128, 128), 0) == lax.broadcasted_iota(
        jnp.int32, (128, 128), 1
    )

    def column(row):
        return jnp.sum(jnp.where(eye, jnp.broadcast_to(row, (128, 128)), 0.0), axis=1, keepdims=True)

    lane = lax.broadcasted_iota(jnp.int32, (128, 128), 1).astype(F32)
    doc_col = column(docs[...].astype(F32)) + 64.0
    stream_col = column(streams[...].astype(F32))
    m_buf[c] = jnp.where(
        lane < 64.0, jnp.where(lane == stream_col, 1.0, 0.0), jnp.where(lane == doc_col, 1.0, 0.0)
    )
    m_recv = remote(m_buf.at[c], m_buf.at[c], sibling)

    def cols(h):
        return pl.ds(h * 256, 256)

    for j in range(1, NC):
        b_recv.append(send_b(j))
    st_recv = remote(st_buf.at[c], st_buf.at[c], sibling)
    nd_side = Group(nd_buf.at[:, c])

    def pass_on(k):
        whole = nd_buf.at[(z + k) % 4, c]
        nd_side.send(whole, whole, sibling)

    pass_on(0)

    for i in range(16):
        stat_buf[0, i : i + 1, :] = sq_buf[i, 0:1, :]
    own_counts = jnp.sum(m_buf[c], axis=0, keepdims=True)
    stat_buf[0, 16:24, :] = jnp.broadcast_to(own_counts, (8, 128))
    stat_c = remote(stat_buf.at[0], statr_buf.at[0], sibling)

    def part(k, h):
        return ((y + k) % 4) * 2 + h

    r1 = [None] * NC
    r2 = [None] * NC

    def stage_a(j):
        slot = j % SLOTS
        if j >= SLOTS:
            r1[j - SLOTS].wait_send()
            r2[j - SLOTS].wait_send()
        b_load[j].wait()
        b_recv[j].wait_recv()
        r1[j] = Group(r1_buf.at[j])
        r2[j] = Group(r2_buf.at[j])

        def body(i, _):
            if j == 0:
                for n in range(4):

                    @pl.when(i == 2 * n)
                    def _(n=n):
                        a_recv[n].wait_recv()

            b = (y * 2 + 4 + i) % 8
            acc = jnp.dot(a_buf[0, b], b_buf[0, j].reshape(1024, 512), preferred_element_type=F32)
            acc = acc + jnp.dot(
                a_buf[1, b], b_buf[1, j].reshape(1024, 512), preferred_element_type=F32
            )
            p_buf[slot, b] = acc.astype(BF)

            @pl.when(i == 0)
            def _():
                r1[j].send(p_buf.at[slot, part(2, 0)], r1_buf.at[j, 0], at_y(1))

            @pl.when(i == 1)
            def _():
                r1[j].send(p_buf.at[slot, part(2, 1)], r1_buf.at[j, 1], at_y(3))

            @pl.when(i == 2)
            def _():
                r2[j].send(p_buf.at[slot, part(3, 0)], r2_buf.at[j, 1, 0], at_y(3))

            @pl.when(i == 7)
            def _():
                r2[j].send(p_buf.at[slot, part(1, 1)], r2_buf.at[j, 0, 1], at_y(1))

            return 0

        lax.fori_loop(0, 8, body, 0)

    def stage_b(j):
        slot = j % SLOTS
        r1[j].wait_recv()
        for i, (k, h) in enumerate(((1, 0), (3, 1))):
            b = part(k, h)
            p_buf[slot, b] = (p_buf[slot, b].astype(F32) + r1_buf[j, i].astype(F32)).astype(BF)
            r2[j].send(p_buf.at[slot, b], r2_buf.at[j, i, h], at_y(k))

    def summed(j, h, lanes):
        slot = j % SLOTS
        return (
            p_buf[slot, part(0, h), :, lanes].astype(F32)
            + r2_buf[j, 0, h, :, lanes].astype(F32)
            + r2_buf[j, 1, h, :, lanes].astype(F32)
        )

    rx = [None] * NC

    def stage_c(j):
        r2[j].wait_recv()
        for i in range(4):
            lanes = pl.ds(i * 128, 128)
            sx_buf[j, :, lanes] = summed(j, 1 - xl, lanes).astype(BF)
        rx[j] = remote(sx_buf.at[j], rx_buf.at[j], x_pair)
        for i in range(4):
            lanes = pl.ds(i * 128, 128)
            own_buf[j % 2, :, lanes] = summed(j, xl, lanes)

    gr = [None] * NC

    def stage_d(j):
        rx[j].wait_recv()
        gr[j] = Group(gr_buf.at[j, pl.ds(0, 3)])
        for yp in range(4):
            lanes = pl.ds(yp * 128, 128)
            target = own_buf[j % 2, :, lanes] + rx_buf[j, :, lanes].astype(F32)
            lane0 = yp * 1024 + (j // 2) * 512 + (j % 2) * 128 + c * 256
            st = st_buf[:, :, pl.ds(pl.multiple_of(lane0, 128), 128)].reshape(256, 128)
            hidden = hr_buf[j // 2, yp, :, pl.ds((j % 2) * 128, 128)]
            error = st.astype(F32) + hidden.astype(F32) - target * rs_buf[...]
            if j == 0 and yp == 0:
                te_buf[...] = error * error
            else:
                te_buf[...] += error * error
            gs_buf[j, yp] = (error * sc_buf[...]).astype(BF)
        for k in (2, 1, 3):
            gr[j].send(gs_buf.at[j, (z + k) % 4], gr_buf.at[j, z], at_z(k))
        gr_buf[j, z] = gs_buf[j, z]

    d1 = [None] * NC
    d2 = [None] * NC

    def dpart(k, h):
        return ((x + k) % 4) * 2 + h

    def stage_e(j):
        gr[j].wait_recv()
        gt_buf[...] = gr_buf[j].reshape(1024, 128).T
        d1[j] = Group(dr1_buf.at[j])
        d2[j] = Group(dr2_buf.at[j])

        def body(i, _):
            b = (x * 2 + 4 + i) % 8
            lanes = pl.ds(pl.multiple_of(b * 512, 512), 512)
            nd = nd_buf[:, :, :, lanes].reshape(1024, 512)
            b_buf[0, j, b] = jnp.dot(gt_buf[...], nd, preferred_element_type=F32).astype(BF)

            @pl.when(i == 0)
            def _():
                d1[j].send(b_buf.at[0, j, dpart(2, 0)], dr1_buf.at[j, 0], at_x(1))

            @pl.when(i == 1)
            def _():
                d1[j].send(b_buf.at[0, j, dpart(2, 1)], dr1_buf.at[j, 1], at_x(3))

            @pl.when(i == 2)
            def _():
                d2[j].send(b_buf.at[0, j, dpart(3, 0)], dr2_buf.at[j, 1, 0], at_x(3))

            @pl.when(i == 7)
            def _():
                d2[j].send(b_buf.at[0, j, dpart(1, 1)], dr2_buf.at[j, 0, 1], at_x(1))

            return 0

        lax.fori_loop(0, 8, body, 0)

    def stage_f(j):
        d1[j].wait_recv()
        for i, (k, h) in enumerate(((1, 0), (3, 1))):
            b = dpart(k, h)
            b_buf[0, j, b] = (b_buf[0, j, b].astype(F32) + dr1_buf[j, i].astype(F32)).astype(BF)
            d2[j].send(b_buf.at[0, j, b], dr2_buf.at[j, i, h], at_x(k))

    dy = [None] * NC

    def stage_g(j):
        d2[j].wait_recv()
        for zp in range(4):
            h, lanes = zp // 2, pl.ds((zp % 2) * 256, 256)
            ds_buf[j, zp] = (
                b_buf[0, j, dpart(0, h), :, lanes].astype(F32)
                + dr2_buf[j, 0, h, :, lanes].astype(F32)
                + dr2_buf[j, 1, h, :, lanes].astype(F32)
            ).astype(BF)
        dy[j] = Group(dy_buf.at[j, pl.ds(0, 3)])
        for k in (2, 1, 3):
            dy[j].send(ds_buf.at[j, (y + k) % 4], dy_buf.at[j, y], at_y(k))

    final = [None] * NC

    def stage_h(j):
        dy[j].wait_recv()
        total = ds_buf[j, y].astype(F32)
        for k in (1, 2, 3):
            total = total + dy_buf[j, (y + k) % 4].astype(F32)
        fs_buf[j] = total.astype(BF)
        final[j] = crossed(
            fs_buf.at[j],
            fr_buf.at[j % 2, xl],
            device(xh, y, z, j // 2, c),
            jnp.logical_and(y == z, xl == j // 2),
            2 + 2 * (j % 2),
        )

    w_x = [None, None]

    def gather_x1(h):
        own = w_buf.at[x, :, :, cols(h)]
        pltpu.make_async_copy(own, own, cross_sem.at[h]).wait()
        w_x[h] = Group(w_buf.at[pl.ds(0, 2), :, :, cols(h)])
        for k in (1, 3):
            w_x[h].send(own, own, at_x(k))

    w_f = [None, None]

    def gather_x2(h):
        w_x[h].wait_recv()
        w_f[h] = Group(w_buf.at[0, :, :, cols(h)])
        left = w_buf.at[(x + 3) % 4, pl.ds(0, 2), :, cols(h)]
        w_f[h].send(left, left, at_x(1))
        right = w_buf.at[(x + 1) % 4, pl.ds(2, 2), :, cols(h)]
        w_f[h].send(right, right, at_x(3))

    hr = [None, None]

    def hidden_half(h):
        w_f[h].wait_recv()
        hr[h] = Group(hr_buf.at[h, pl.ds(0, 3)])

        def body(i, _):
            zd = (z + 1 + i) % 4
            hs_buf[h, zd] = jnp.dot(
                nd_buf[zd].reshape(256, D),
                w_buf[:, :, :, cols(h)].reshape(D, 256),
                preferred_element_type=F32,
            ).astype(BF)

            @pl.when(i < 3)
            def _():
                hr[h].send(hs_buf.at[h, zd], hr_buf.at[h, z], device(xh, zd, y, xl, c))

            return 0

        lax.fori_loop(0, 4, body, 0)
        hr_buf[h, z] = hs_buf[h, z]

    def loss_of(core):
        rows = pl.ds(core * 128, 128)
        te = jnp.sum(te_buf[rows], axis=1, keepdims=True) / D
        return jnp.sum(m_buf[core] * (te / ln_buf[rows]), axis=0, keepdims=True)

    stage_a(0)
    gather_x1(0)
    gather_x1(1)
    nd_right[0].wait_recv()
    nd_far = Group(nd_buf.at[z, c])
    from_left = nd_buf.at[(z + 3) % 4, c, half(0)]
    nd_far.send(from_left, from_left, at_z(1))
    nd_left[1].wait_recv()
    from_right = nd_buf.at[(z + 1) % 4, c, half(1)]
    nd_far.send(from_right, from_right, at_z(3))
    stat_c.wait_recv()
    stat_buf[1] = stat_buf[0] + statr_buf[0]
    stat_x = remote(stat_buf.at[1], statr_buf.at[1], x_pair)
    stage_a(1)
    stat_x.wait_recv()
    stat_buf[2] = stat_buf[1] + statr_buf[1]
    stat_y = Group(staty_buf.at[pl.ds(0, 3)])
    for k in (1, 2, 3):
        stat_y.send(stat_buf.at[2], staty_buf.at[y], at_y(k))
    staty_buf[y] = stat_buf[2]
    stage_b(0)
    stage_a(2)
    gather_x2(0)
    stat_y.wait_recv()
    stat = staty_buf[0] + staty_buf[1] + staty_buf[2] + staty_buf[3]
    stat_buf[3] = stat
    statz_buf[z] = stat[16:24]
    stat_z = Group(statz_buf.at[pl.ds(0, 3)])
    for k in (1, 2, 3):
        stat_z.send(stat_buf.at[3, pl.ds(16, 8)], statz_buf.at[z], at_z(k))
    nd_right[1].wait_recv()
    nd_left[0].wait_recv()
    pass_on(3)
    pass_on(1)
    stage_b(1)
    stage_c(0)
    stage_a(3)
    stat_z.wait_recv()
    stato_buf[0] = statz_buf[0] + statz_buf[1] + statz_buf[2] + statz_buf[3]
    stat_o = remote(stato_buf.at[0], stato_buf.at[1], x_outer)
    gather_x2(1)
    nd_far.wait_recv()
    pass_on(2)
    stage_b(2)

    stat_o.wait_recv()
    m_recv.wait_recv()
    lane1 = lax.broadcasted_iota(jnp.int32, (8, 128), 1)
    doc_counts = jnp.where(lane1 >= 64, stato_buf[0] + stato_buf[1], 0.0)[0:1]
    stream_w = jnp.zeros((8, 128), F32)
    for i in range(8):
        stream_w = jnp.where(lane1 == i, wstream[i], stream_w)
    stream_w = stream_w[0:1]
    rows_i = lax.broadcasted_iota(jnp.int32, (24, 128), 0)
    for core in range(2):
        rows = pl.ds(core * 128, 128)
        row = jnp.sum(
            jnp.where(rows_i == (y * 2 + xl) * 2 + core, stat_buf[3], 0.0), axis=0, keepdims=True
        )
        rs_buf[rows] = jnp.broadcast_to(lax.rsqrt(column(row) / DT + EPS), (128, 128))
        m = m_buf[core]
        length = jnp.sum(m * doc_counts, axis=1, keepdims=True)
        sw = jnp.sum(m * stream_w, axis=1, keepdims=True)
        sc_buf[rows] = jnp.broadcast_to(2.0 * sw / length, (128, 128))
        ln_buf[rows] = jnp.broadcast_to(length, (128, 128))
    st_recv.wait_recv()

    nd_side.wait_recv()
    hidden_half(0)
    stage_c(1)
    stage_b(3)
    hr[0].wait_recv()
    stage_d(0)
    stage_d(1)
    hidden_half(1)
    stage_e(0)
    stage_e(1)
    stage_f(0)
    stage_c(2)
    hr[1].wait_recv()
    stage_d(2)
    stage_f(1)
    stage_e(2)
    stage_c(3)
    stage_f(2)
    stage_g(0)
    stage_g(1)
    stage_d(3)
    loss_buf[0] = jnp.broadcast_to(loss_of(0) + loss_of(1), (8, 128))
    loss_c = remote(loss_buf.at[0], lossr_buf.at[0], sibling)
    stage_h(0)
    stage_e(3)
    stage_g(2)
    stage_h(1)
    loss_c.wait_recv()
    loss_buf[1] = loss_buf[0] + lossr_buf[0]
    loss_x = remote(loss_buf.at[1], lossr_buf.at[1], x_pair)
    stage_f(3)
    stage_h(2)
    loss_x.wait_recv()
    loss_buf[2] = loss_buf[1] + lossr_buf[1]
    lossr_buf[4 + y] = loss_buf[2]
    loss_y = Group(lossr_buf.at[pl.ds(4, 3)])
    for k in (1, 2, 3):
        loss_y.send(loss_buf.at[2], lossr_buf.at[4 + y], at_y(k))
    stage_g(3)
    loss_y.wait_recv()
    loss_buf[3] = lossr_buf[4] + lossr_buf[5] + lossr_buf[6] + lossr_buf[7]
    lossr_buf[8 + z] = loss_buf[3]
    loss_z = Group(lossr_buf.at[pl.ds(8, 3)])
    for k in (1, 2, 3):
        loss_z.send(loss_buf.at[3], lossr_buf.at[8 + z], at_z(k))
    stage_h(3)
    loss_z.wait_recv()
    loss_buf[4] = lossr_buf[8] + lossr_buf[9] + lossr_buf[10] + lossr_buf[11]
    loss_o = remote(loss_buf.at[4], lossr_buf.at[2], x_outer)
    for group in list(open_sends):
        group.wait_send()
    for pair in w_swap + final:
        crossed_sent(pair)
    loss_o.wait_recv()
    out_loss[...] = (loss_buf[4] + lossr_buf[2])[0:1, 0:8]

    for jj in range(2):
        for r in range(2):
            got = fr_buf.at[jj, r]
            pltpu.make_async_copy(got, got, cross_sem.at[2 + 2 * jj + r]).wait()
            out_grad[pl.ds(r * 256, 256), pl.ds(jj * 128, 128)] = fr_buf[jj, r].astype(F32).T
    assert used[0] <= SEMS, used[0]


def shards(
    teacher_hidden,
    teacher_gain,
    target_proj,
    student_in,
    student_gain,
    proj_weight,
    doc_ids,
    stream_ids,
    stream_weight,
):
    hbm = pl.BlockSpec(memory_space=pl.ANY)
    vmem = pl.BlockSpec(memory_space=pltpu.VMEM)
    scratch = [
        ((2, 8, 256, 1024), BF),
        ((2, NC, 8, 128, 512), BF),
        ((SLOTS, 8, 256, 512), BF),
        ((NC, 2, 256, 512), BF),
        ((NC, 2, 2, 256, 512), BF),
        ((NC, 256, 512), BF),
        ((NC, 256, 512), BF),
        ((4, 2, 128, D), BF),
        ((4, 4, 256, 512), BF),
        ((2, 4, 256, 256), BF),
        ((2, 4, 256, 256), BF),
        ((2, 128, D), BF),
        ((NC, 4, 256, 128), BF),
        ((NC, 4, 256, 128), BF),
        ((128, 1024), BF),
        ((NC, 2, 128, 512), BF),
        ((NC, 2, 2, 128, 512), BF),
        ((NC, 4, 128, 256), BF),
        ((NC, 4, 128, 256), BF),
        ((NC, 128, 256), BF),
        ((2, 2, 128, 256), BF),
        ((2, 128, 128), F32),
        ((16, 8, 128), F32),
        ((4, 24, 128), F32),
        ((2, 24, 128), F32),
        ((4, 24, 128), F32),
        ((4, 8, 128), F32),
        ((2, 8, 128), F32),
        ((5, 8, 128), F32),
        ((12, 8, 128), F32),
        ((256, 128), F32),
        ((256, 128), F32),
        ((256, 128), F32),
        ((256, 128), F32),
        ((2, 256, 512), F32),
    ]
    w_grad, loss = pl.pallas_call(
        kernel,
        out_shape=(
            jax.ShapeDtypeStruct((512, 256), F32),
            jax.ShapeDtypeStruct((1, 8), F32),
        ),
        in_specs=[hbm, vmem, hbm, hbm, vmem, hbm, vmem, vmem, pl.BlockSpec(memory_space=pltpu.SMEM)],
        out_specs=(vmem, vmem),
        scratch_shapes=[pltpu.VMEM(shape, kind) for shape, kind in scratch]
        + [pltpu.SemaphoreType.DMA((SEMS,)), pltpu.SemaphoreType.DMA((6,))],
        compiler_params=pltpu.CompilerParams(
            collective_id=0, has_side_effects=True, vmem_limit_bytes=62 * 2**20
        ),
        cost_estimate=pl.CostEstimate(flops=26 * 10**9, bytes_accessed=16 * 2**20, transcendentals=0),
    )(
        teacher_hidden.reshape(8, 256, 1024),
        teacher_gain.reshape(8, 128),
        target_proj.reshape(8, 128, D),
        student_in,
        student_gain.reshape(D // 128, 128),
        proj_weight,
        doc_ids.reshape(1, 128),
        stream_ids.reshape(1, 128),
        stream_weight,
    )
    return loss.reshape(8), w_grad


def solution(mesh):
    in_specs = (
        P("seq", "tp"),
        P("tp"),
        P("tp", None),
        P(("seq", "tp"), None),
        P(),
        P("seq", "tp"),
        P(("seq", "tp")),
        P(("seq", "tp")),
        P(),
    )
    out_specs = (P(), P("seq", "tp"))
    return jax.shard_map(shards, mesh=mesh, in_specs=in_specs, out_specs=out_specs, check_vma=False)
```

time: 169 us -> 157 us (0.929)
  Pallas kernels: 158 us -> 153 us
  local copies, waits for them, and re-layouts: 6.16 us -> 2.97 us
  other arithmetic: 2.41 us -> 0 us
    pallas_call x1, Pallas kernels: 158 us -> 153 us  [shards(): pl.pallas_call(kernel, out_shape=(jax.ShapeDtypeStruct((512, 256), F32),...]
    reshape x2 -> x0, local copies, waits for them, and re-layouts: 2.58 us -> none  [the longest x1 1.3 us: shards(): student_gain.reshape(1, D)]
    convert_element_type x2 -> x0, other arithmetic: 2.4 us -> none  [the longest x1 1.4 us: shards(): meta = jnp.where(lane < 64, doc_ids[:, None] == lane, stream_ids[:, None]...]
    unnamed x1 -> x2, local copies, waits for them, and re-layouts: 1 us -> 2.97 us
where the time goes in v2:
time: 157 us; the launch traced here: 156 us
  Pallas kernels  153 us (97%)
  local copies, waits for them, and re-layouts  2.97 us (2%)
    pallas_call x1, Pallas kernels, shards(): pl.pallas_call(kernel, out_shape=(jax.ShapeDtypeStruct((512, 256), F32),...  153 us

profile of v2, /device:TPU:0, one launch (start us, length us, event | category | flops | bytes accessed | tf_op | source)
XLA Modules:
  0.0 156.4 jit_solution(12826597943803253940)
XLA Ops:
  0.6 152.8 %shard_map.104 = (f32[512,256]{1,0:T(8,128)}, f32[1,8]{1,0:T(1,128)}) custom-call(bf16[8,256,1024]{2,1,0:T(8,128)(2,1)} %bitcast.8, bf16[8,128]{1,0:T(8,128)(2,1)} %bitcast.10, bf16[8,128,4096]{2,1,0:T(8,128)(2,1)} %bitcast.7, bf16[128,4096]{1,0:T(8,128)(2,1)} %student.1, bf16[32,128]{1,0:T(8,128)(2,1)} %bitcast.9, bf16[512,256]{1,0:T(8,128)(2,1)} %weight.1, ...), custom_call_target="tpu_custom_call" | custom-call | flops 25999998976 | bytes 16777216 | tf_op jit(solution)/shard_map/pallas_call | solution.py:714
  153.4 1.1 copy.13
  154.5 1.9 %copy.14 = f32[512,256]{1,0:T(8,128)} copy(f32[512,256]{1,0:T(8,128)} %get-tuple-element.9) | data formatting | bytes 1048576

commit v3 on v2

--- a/solution.py
+++ b/solution.py
@@ -14,6 +14,13 @@
 BF = jnp.bfloat16
 F32 = jnp.float32
 MESH = pl.DeviceIdType.MESH
+SCHEDULE = (
+    "A0", "X0", "X1", "N1", "S1", "A1", "S2", "B0", "A2", "Y0", "S3", "N2",
+    "B1", "C0", "A3", "S4", "Y1", "N3", "B2", "S5", "N4", "Q0", "C1", "B3",
+    "R0", "D0", "Q1", "E0", "D1", "F0", "C2", "E1", "R1", "D2", "F1", "C3",
+    "E2", "G0", "F2", "D3", "L1", "G1", "H0", "E3", "G2", "H1", "L2", "F3",
+    "H2", "L3", "G3", "L4", "H3", "L5",
+)
 
 
 def device(xh, z, y, xl, c):
@@ -530,127 +537,151 @@
         te = jnp.sum(te_buf[rows], axis=1, keepdims=True) / D
         return jnp.sum(m_buf[core] * (te / ln_buf[rows]), axis=0, keepdims=True)
 
-    stage_a(0)
-    gather_x1(0)
-    gather_x1(1)
-    nd_right[0].wait_recv()
-    nd_far = Group(nd_buf.at[z, c])
-    from_left = nd_buf.at[(z + 3) % 4, c, half(0)]
-    nd_far.send(from_left, from_left, at_z(1))
-    nd_left[1].wait_recv()
-    from_right = nd_buf.at[(z + 1) % 4, c, half(1)]
-    nd_far.send(from_right, from_right, at_z(3))
-    stat_c.wait_recv()
-    stat_buf[1] = stat_buf[0] + statr_buf[0]
-    stat_x = remote(stat_buf.at[1], statr_buf.at[1], x_pair)
-    stage_a(1)
-    stat_x.wait_recv()
-    stat_buf[2] = stat_buf[1] + statr_buf[1]
-    stat_y = Group(staty_buf.at[pl.ds(0, 3)])
-    for k in (1, 2, 3):
-        stat_y.send(stat_buf.at[2], staty_buf.at[y], at_y(k))
-    staty_buf[y] = stat_buf[2]
-    stage_b(0)
-    stage_a(2)
-    gather_x2(0)
-    stat_y.wait_recv()
-    stat = staty_buf[0] + staty_buf[1] + staty_buf[2] + staty_buf[3]
-    stat_buf[3] = stat
-    statz_buf[z] = stat[16:24]
-    stat_z = Group(statz_buf.at[pl.ds(0, 3)])
-    for k in (1, 2, 3):
-        stat_z.send(stat_buf.at[3, pl.ds(16, 8)], statz_buf.at[z], at_z(k))
-    nd_right[1].wait_recv()
-    nd_left[0].wait_recv()
-    pass_on(3)
-    pass_on(1)
-    stage_b(1)
-    stage_c(0)
-    stage_a(3)
-    stat_z.wait_recv()
-    stato_buf[0] = statz_buf[0] + statz_buf[1] + statz_buf[2] + statz_buf[3]
-    stat_o = remote(stato_buf.at[0], stato_buf.at[1], x_outer)
-    gather_x2(1)
-    nd_far.wait_recv()
-    pass_on(2)
-    stage_b(2)
-
-    stat_o.wait_recv()
-    m_recv.wait_recv()
-    lane1 = lax.broadcasted_iota(jnp.int32, (8, 128), 1)
-    doc_counts = jnp.where(lane1 >= 64, stato_buf[0] + stato_buf[1], 0.0)[0:1]
-    stream_w = jnp.zeros((8, 128), F32)
-    for i in range(8):
-        stream_w = jnp.where(lane1 == i, wstream[i], stream_w)
-    stream_w = stream_w[0:1]
-    rows_i = lax.broadcasted_iota(jnp.int32, (24, 128), 0)
-    for core in range(2):
-        rows = pl.ds(core * 128, 128)
-        row = jnp.sum(
-            jnp.where(rows_i == (y * 2 + xl) * 2 + core, stat_buf[3], 0.0), axis=0, keepdims=True
-        )
-        rs_buf[rows] = jnp.broadcast_to(lax.rsqrt(column(row) / DT + EPS), (128, 128))
-        m = m_buf[core]
-        length = jnp.sum(m * doc_counts, axis=1, keepdims=True)
-        sw = jnp.sum(m * stream_w, axis=1, keepdims=True)
-        sc_buf[rows] = jnp.broadcast_to(2.0 * sw / length, (128, 128))
-        ln_buf[rows] = jnp.broadcast_to(length, (128, 128))
-    st_recv.wait_recv()
-
-    nd_side.wait_recv()
-    hidden_half(0)
-    stage_c(1)
-    stage_b(3)
-    hr[0].wait_recv()
-    stage_d(0)
-    stage_d(1)
-    hidden_half(1)
-    stage_e(0)
-    stage_e(1)
-    stage_f(0)
-    stage_c(2)
-    hr[1].wait_recv()
-    stage_d(2)
-    stage_f(1)
-    stage_e(2)
-    stage_c(3)
-    stage_f(2)
-    stage_g(0)
-    stage_g(1)
-    stage_d(3)
-    loss_buf[0] = jnp.broadcast_to(loss_of(0) + loss_of(1), (8, 128))
-    loss_c = remote(loss_buf.at[0], lossr_buf.at[0], sibling)
-    stage_h(0)
-    stage_e(3)
-    stage_g(2)
-    stage_h(1)
-    loss_c.wait_recv()
-    loss_buf[1] = loss_buf[0] + lossr_buf[0]
-    loss_x = remote(loss_buf.at[1], lossr_buf.at[1], x_pair)
-    stage_f(3)
-    stage_h(2)
-    loss_x.wait_recv()
-    loss_buf[2] = loss_buf[1] + lossr_buf[1]
-    lossr_buf[4 + y] = loss_buf[2]
-    loss_y = Group(lossr_buf.at[pl.ds(4, 3)])
-    for k in (1, 2, 3):
-        loss_y.send(loss_buf.at[2], lossr_buf.at[4 + y], at_y(k))
-    stage_g(3)
-    loss_y.wait_recv()
-    loss_buf[3] = lossr_buf[4] + lossr_buf[5] + lossr_buf[6] + lossr_buf[7]
-    lossr_buf[8 + z] = loss_buf[3]
-    loss_z = Group(lossr_buf.at[pl.ds(8, 3)])
-    for k in (1, 2, 3):
-        loss_z.send(loss_buf.at[3], lossr_buf.at[8 + z], at_z(k))
-    stage_h(3)
-    loss_z.wait_recv()
-    loss_buf[4] = lossr_buf[8] + lossr_buf[9] + lossr_buf[10] + lossr_buf[11]
-    loss_o = remote(loss_buf.at[4], lossr_buf.at[2], x_outer)
+    far = Group(nd_buf.at[z, c])
+
+    def rows_second():
+        nd_right[0].wait_recv()
+        from_left = nd_buf.at[(z + 3) % 4, c, half(0)]
+        far.send(from_left, from_left, at_z(1))
+        nd_left[1].wait_recv()
+        from_right = nd_buf.at[(z + 1) % 4, c, half(1)]
+        far.send(from_right, from_right, at_z(3))
+
+    def rows_near():
+        nd_right[1].wait_recv()
+        nd_left[0].wait_recv()
+        pass_on(3)
+        pass_on(1)
+
+    def rows_far():
+        far.wait_recv()
+        pass_on(2)
+
+    kept = {}
+
+    def stat_1():
+        stat_c.wait_recv()
+        stat_buf[1] = stat_buf[0] + statr_buf[0]
+        kept["x"] = remote(stat_buf.at[1], statr_buf.at[1], x_pair)
+
+    def stat_2():
+        kept["x"].wait_recv()
+        stat_buf[2] = stat_buf[1] + statr_buf[1]
+        kept["y"] = Group(staty_buf.at[pl.ds(0, 3)])
+        for k in (1, 2, 3):
+            kept["y"].send(stat_buf.at[2], staty_buf.at[y], at_y(k))
+        staty_buf[y] = stat_buf[2]
+
+    def stat_3():
+        kept["y"].wait_recv()
+        stat = staty_buf[0] + staty_buf[1] + staty_buf[2] + staty_buf[3]
+        stat_buf[3] = stat
+        statz_buf[z] = stat[16:24]
+        kept["z"] = Group(statz_buf.at[pl.ds(0, 3)])
+        for k in (1, 2, 3):
+            kept["z"].send(stat_buf.at[3, pl.ds(16, 8)], statz_buf.at[z], at_z(k))
+
+    def stat_4():
+        kept["z"].wait_recv()
+        stato_buf[0] = statz_buf[0] + statz_buf[1] + statz_buf[2] + statz_buf[3]
+        kept["o"] = remote(stato_buf.at[0], stato_buf.at[1], x_outer)
+
+    def scales():
+        kept["o"].wait_recv()
+        m_recv.wait_recv()
+        lane1 = lax.broadcasted_iota(jnp.int32, (8, 128), 1)
+        doc_counts = jnp.where(lane1 >= 64, stato_buf[0] + stato_buf[1], 0.0)[0:1]
+        stream_w = jnp.zeros((8, 128), F32)
+        for i in range(8):
+            stream_w = jnp.where(lane1 == i, wstream[i], stream_w)
+        stream_w = stream_w[0:1]
+        rows_i = lax.broadcasted_iota(jnp.int32, (24, 128), 0)
+        for core in range(2):
+            rows = pl.ds(core * 128, 128)
+            row = jnp.sum(
+                jnp.where(rows_i == (y * 2 + xl) * 2 + core, stat_buf[3], 0.0),
+                axis=0,
+                keepdims=True,
+            )
+            rs_buf[rows] = jnp.broadcast_to(lax.rsqrt(column(row) / DT + EPS), (128, 128))
+            m = m_buf[core]
+            length = jnp.sum(m * doc_counts, axis=1, keepdims=True)
+            sw = jnp.sum(m * stream_w, axis=1, keepdims=True)
+            sc_buf[rows] = jnp.broadcast_to(2.0 * sw / length, (128, 128))
+            ln_buf[rows] = jnp.broadcast_to(length, (128, 128))
+        st_recv.wait_recv()
+
+    def loss_1():
+        loss_buf[0] = jnp.broadcast_to(loss_of(0) + loss_of(1), (8, 128))
+        kept["lc"] = remote(loss_buf.at[0], lossr_buf.at[0], sibling)
+
+    def loss_2():
+        kept["lc"].wait_recv()
+        loss_buf[1] = loss_buf[0] + lossr_buf[0]
+        kept["lx"] = remote(loss_buf.at[1], lossr_buf.at[1], x_pair)
+
+    def loss_3():
+        kept["lx"].wait_recv()
+        loss_buf[2] = loss_buf[1] + lossr_buf[1]
+        lossr_buf[4 + y] = loss_buf[2]
+        kept["ly"] = Group(lossr_buf.at[pl.ds(4, 3)])
+        for k in (1, 2, 3):
+            kept["ly"].send(loss_buf.at[2], lossr_buf.at[4 + y], at_y(k))
+
+    def loss_4():
+        kept["ly"].wait_recv()
+        loss_buf[3] = lossr_buf[4] + lossr_buf[5] + lossr_buf[6] + lossr_buf[7]
+        lossr_buf[8 + z] = loss_buf[3]
+        kept["lz"] = Group(lossr_buf.at[pl.ds(8, 3)])
+        for k in (1, 2, 3):
+            kept["lz"].send(loss_buf.at[3], lossr_buf.at[8 + z], at_z(k))
+
+    def loss_5():
+        kept["lz"].wait_recv()
+        loss_buf[4] = lossr_buf[8] + lossr_buf[9] + lossr_buf[10] + lossr_buf[11]
+        kept["lo"] = remote(loss_buf.at[4], lossr_buf.at[2], x_outer)
+
+    by_chunk = {
+        "A": stage_a,
+        "B": stage_b,
+        "C": stage_c,
+        "D": stage_d,
+        "E": stage_e,
+        "F": stage_f,
+        "G": stage_g,
+        "H": stage_h,
+        "X": gather_x1,
+        "Y": gather_x2,
+        "Q": hidden_half,
+        "R": lambda h: hr[h].wait_recv(),
+    }
+    once = {
+        "N1": rows_second,
+        "N2": rows_near,
+        "N3": rows_far,
+        "N4": nd_side.wait_recv,
+        "S1": stat_1,
+        "S2": stat_2,
+        "S3": stat_3,
+        "S4": stat_4,
+        "S5": scales,
+        "L1": loss_1,
+        "L2": loss_2,
+        "L3": loss_3,
+        "L4": loss_4,
+        "L5": loss_5,
+    }
+    for step in SCHEDULE:
+        if step in once:
+            once[step]()
+        else:
+            by_chunk[step[0]](int(step[1]))
+
     for group in list(open_sends):
         group.wait_send()
     for pair in w_swap + final:
         crossed_sent(pair)
-    loss_o.wait_recv()
+    kept["lo"].wait_recv()
     out_loss[...] = (loss_buf[4] + lossr_buf[2])[0:1, 0:8]
 
     for jj in range(2):

time: 157 us -> 157 us (level)
  no operation moved by 1% of the time
where the time goes in v3:
time: 157 us; the launch traced here: 156 us
  Pallas kernels  152 us (97%)
  local copies, waits for them, and re-layouts  2.97 us (2%)
    pallas_call x1, Pallas kernels, shards(): pl.pallas_call(kernel, out_shape=(jax.ShapeDtypeStruct((512, 256), F32),...  152 us

profile of v3, /device:TPU:0, one launch (start us, length us, event | category | flops | bytes accessed | tf_op | source)
XLA Modules:
  0.0 155.6 jit_solution(11126570109852954414)
XLA Ops:
  0.6 152.0 %shard_map.104 = (f32[512,256]{1,0:T(8,128)}, f32[1,8]{1,0:T(1,128)}) custom-call(bf16[8,256,1024]{2,1,0:T(8,128)(2,1)} %bitcast.8, bf16[8,128]{1,0:T(8,128)(2,1)} %bitcast.10, bf16[8,128,4096]{2,1,0:T(8,128)(2,1)} %bitcast.7, bf16[128,4096]{1,0:T(8,128)(2,1)} %student.1, bf16[32,128]{1,0:T(8,128)(2,1)} %bitcast.9, bf16[512,256]{1,0:T(8,128)(2,1)} %weight.1, ...), custom_call_target="tpu_custom_call" | custom-call | flops 25999998976 | bytes 16777216 | tf_op jit(solution)/shard_map/pallas_call | solution.py:745
  152.6 1.1 copy.13
  153.7 1.9 %copy.14 = f32[512,256]{1,0:T(8,128)} copy(f32[512,256]{1,0:T(8,128)} %get-tuple-element.9) | data formatting | bytes 1048576
